TPU v7x, 32 devices: a whole 2x2x4 slice. The times are simulated.
32 devices in a mesh: visit: 4 (over z), patch: 8 (over y, x, core).
Axes of the slice: x: 2, y: 2, z: 4, core: 2. Of those that a mesh axis runs over, the one named last changes fastest.
Arguments:
- ccd_images: bfloat16 [128, 512, 256], P(('visit', 'patch')), may hold values from -6 to 6
- ccd_weight: float32 [128], replicated, may hold values from 0.25 to 4
- psf_index: int32 [128], replicated, may hold values from 0 to 7
- patch_target: int32 [512, 1], replicated, may hold values from 0 to 7; in each aligned block of 16 rows (0 to 15, 16 to 31, ...) at most 2 rows name the same one
- tile_slot: int32 [512], replicated, may hold values from 0 to 15
- row_matrix: int32 [512], replicated, may hold values from 0 to 7
- col_matrix: int32 [512], replicated, may hold values from 0 to 7
- warp_rows: bfloat16 [8, 256, 512], replicated, may hold values from -0.25 to 0.25
- warp_cols: bfloat16 [8, 256, 256], replicated, may hold values from -0.375 to 0.375
- psf_match: bfloat16 [8, 256, 256], replicated, may hold values from -0.375 to 0.375
- detect_kernel: float32 [9], replicated, may hold values from 0.2 to 1
Outputs:
- coadd: float32 [1024, 8192], P('visit', 'patch')
- detection: float32 [1024, 8192], P('visit', 'patch')
Inputs may be any that keep to these rules, and one draw needn't show every extreme that they name: `patch_target`: in each aligned block of 16 entries (the entries of one device) no patch is named more than 2 times, a bound that some block reaches.
All inputs are finite; a program needn't handle non-finite values.
Results may differ from a plain program's by a relative error of at most 0.0057.
Values may be sent and summed in bfloat16 or wider, within the bound.
A program may use at most 128 MiB of HBM per device.

v0:
```python
import jax
import jax.numpy as jnp
from jax import lax
from jax.sharding import PartitionSpec as P

K_OV = 4
TS = 256
G = 4
CAP = 2


def extended(block, sides, width):
    for axis, dim in sides:
        count = lax.axis_size(axis)
        forward = [(i, i + 1) for i in range(count - 1)]
        backward = [(target, source) for source, target in forward]
        low = lax.ppermute(
            lax.slice_in_dim(block, block.shape[dim] - width, None, axis=dim), axis, forward
        )
        high = lax.ppermute(lax.slice_in_dim(block, 0, width, axis=dim), axis, backward)
        block = jnp.concatenate([low, block, high], axis=dim)
    return block


def warp_entries(images, row_tables, col_tables, psf_tables):
    first = jnp.einsum(
        "ntc,ncw->ntw", row_tables, images, preferred_element_type=jnp.float32
    ).astype(jnp.bfloat16)
    second = jnp.einsum(
        "ntw,nuw->ntu", first, col_tables, preferred_element_type=jnp.float32
    ).astype(jnp.bfloat16)
    third = jnp.einsum(
        "nst,ntu->nsu", psf_tables, second, preferred_element_type=jnp.float32
    ).astype(jnp.bfloat16)
    return jnp.einsum("nsu,nvu->nsv", third, psf_tables, preferred_element_type=jnp.float32).astype(
        jnp.bfloat16
    )


def slot_positions(targets, n_patch, capacity):
    onehot = (targets[..., :, None] == jnp.arange(n_patch, dtype=jnp.int32)).astype(jnp.int32)
    earlier = jnp.cumsum(onehot, axis=-2) - onehot
    ranking = jnp.sum(earlier * onehot, axis=-1)
    return targets * capacity + ranking


def body(
    ccd_images,
    ccd_weight,
    psf_index,
    patch_target,
    tile_slot,
    row_matrix,
    col_matrix,
    warp_rows,
    warp_cols,
    psf_match,
    detect_kernel,
):
    n_patch = lax.axis_size("patch")
    visit_at = lax.axis_index("visit")
    patch_at = lax.axis_index("patch")
    per_device = ccd_images.shape[0] * K_OV
    slots = n_patch * CAP
    all_targets = patch_target[:, 0]
    entry_ids = jnp.arange(per_device, dtype=jnp.int32)
    own_start = (visit_at * n_patch + patch_at) * per_device
    own_targets = lax.dynamic_slice_in_dim(all_targets, own_start, per_device)
    own_position = slot_positions(own_targets, n_patch, CAP)
    sender_match = (own_position[:, None] == jnp.arange(slots, dtype=jnp.int32)[None, :]).astype(
        jnp.int32
    )
    sender_entry = jnp.sum(sender_match * entry_ids[:, None], axis=0)
    sender_filled = jnp.sum(sender_match, axis=0)
    group_start = visit_at * n_patch * per_device
    group_targets = lax.dynamic_slice_in_dim(
        all_targets, group_start, n_patch * per_device
    ).reshape(n_patch, per_device)
    group_position = slot_positions(group_targets, n_patch, CAP)
    wanted = patch_at * CAP + jnp.arange(CAP, dtype=jnp.int32)
    receiver_match = (group_position[:, :, None] == wanted[None, None, :]).astype(jnp.int32)
    receiver_entry = jnp.sum(receiver_match * entry_ids[None, :, None], axis=1)
    receiver_filled = jnp.sum(receiver_match, axis=1).reshape(slots)
    source_base = group_start + jnp.arange(n_patch, dtype=jnp.int32)[:, None] * per_device
    global_entry = (source_base + receiver_entry).reshape(slots)
    weight_of = jnp.where(receiver_filled > 0, ccd_weight[global_entry // K_OV], 0.0)
    slot_of = tile_slot[global_entry]
    zero_value = jnp.zeros((), jnp.bfloat16)
    outgoing = jnp.where(
        sender_filled[:, None, None] > 0, ccd_images[sender_entry // K_OV], zero_value
    )
    cutouts = lax.all_to_all(
        outgoing.reshape(n_patch, CAP, ccd_images.shape[1], ccd_images.shape[2]),
        "patch",
        split_axis=0,
        concat_axis=0,
        tiled=True,
    )
    cutouts = cutouts.reshape(slots, ccd_images.shape[1], ccd_images.shape[2])
    arrived = warp_entries(
        cutouts,
        warp_rows[row_matrix[global_entry]],
        warp_cols[col_matrix[global_entry]],
        psf_match[psf_index[global_entry // K_OV]],
    )
    selector = jnp.where(
        slot_of[None, :] == jnp.arange(G * G, dtype=jnp.int32)[:, None], weight_of[None, :], 0.0
    )
    summed = jnp.einsum(
        "sb,bx->sx",
        selector,
        arrived.reshape(slots, TS * TS).astype(jnp.float32),
        precision=lax.Precision.HIGHEST,
    )
    partial_value = summed.reshape(G, G, TS, TS).transpose(0, 2, 1, 3).reshape(G * TS, G * TS)
    tile_weights = jnp.sum(selector, axis=1).reshape(G, G)
    pixels = lax.psum_scatter(partial_value, "visit", scatter_dimension=0, tiled=True)
    totals = lax.psum(tile_weights, "visit")
    local_rows = pixels.shape[0]
    row_tile = (visit_at * local_rows + jnp.arange(local_rows, dtype=jnp.int32)) // TS
    picker = row_tile[:, None, None] == jnp.arange(G, dtype=jnp.int32)[None, :, None]
    weight_rows = jnp.sum(jnp.where(picker, totals[None, :, :], 0.0), axis=1)
    coadd = pixels / (1.0 + jnp.repeat(weight_rows, TS, axis=1))
    height = coadd.shape[0]
    width = coadd.shape[1]
    span = detect_kernel.shape[0]
    radius = span // 2
    padded = extended(coadd, (("visit", 0), ("patch", 1)), radius)
    row_pass = detect_kernel[0] * padded[0:height, :]
    for offset in range(1, span):
        row_pass = row_pass + detect_kernel[offset] * padded[offset : offset + height, :]
    detection = detect_kernel[0] * row_pass[:, 0:width]
    for offset in range(1, span):
        detection = detection + detect_kernel[offset] * row_pass[:, offset : offset + width]
    return (coadd, detection)


def solution(mesh):
    in_specs = (P(("visit", "patch"), None, None), P(), P(), P(), P(), P(), P(), P(), P(), P(), P())
    out_specs = (P("visit", "patch"), P("visit", "patch"))
    return jax.shard_map(body, mesh=mesh, in_specs=in_specs, out_specs=out_specs, check_vma=False)
```

profile of v0, /device:TPU:1, one launch (start us, length us, event | category | flops | bytes accessed | tf_op | source)
XLA Modules:
  0.0 216.3 jit_solution(13300005327196378420)
XLA Ops:
  7.2 0.9 fusion.53
  8.2 0.2 select_reduce_fusion.3
  8.4 0.7 fusion.52
  9.1 0.1 convert_reduce_fusion
  9.2 0.7 dynamic-slice_reduce_fusion
  10.0 0.4 fusion.58
  10.5 0.2 fusion.37
  10.8 0.1 copy.29
  11.0 0.1 gt.24
  11.1 4.0 %gather_fusion.6 = bf16[16,512,256]{2,1,0:T(8,128)(2,1)} fusion(bf16[4,512,256]{2,1,0:T(8,128)(2,1)} %param.11, s32[1024]{0:T(1024)S(1)} %pad_clamp_fusion.1), kind=kCustom, calls=%fused_computation.6 | custom fusion | bytes 8388672 | tf_op jit(solution)/shard_map/gather | solution.py:90
  15.0 4.5 %broadcast_select_fusion = bf16[8,2,512,256]{3,2,1,0:T(8,128)(2,1)} fusion(bf16[8,2,512,256]{3,2,1,0:T(8,128)(2,1)} %bitcast.79, pred[8,2]{1,0:T(8,128)(4,1)S(1)} %gt.24), kind=kLoop, calls=%fused_computation.9 | loop fusion | flops 2097152 | bytes 8388624 | tf_op jit(solution)/shard_map/jit(_where)/select_n | solution.py:89
  19.6 5.4 %all-to-all-start = ((bf16[8,2,512,256]{3,2,1,0:T(8,128)(2,1)}), bf16[8,2,512,256]{3,2,1,0:T(8,128)(2,1)}, u32[]{:S(2)}, u32[]{:S(2)}) async-start(bf16[8,2,512,256]{3,2,1,0:T(8,128)(2,1)} %broadcast_select_fusion), calls=%async_computation | async-start | bytes 8388608 | tf_op jit(solution)/shard_map/all_to_all | solution.py:92
  24.9 0.7 gather_fusion.4
  25.6 0.7 gather_fusion.7
  26.3 0.7 gather_fusion.2
  27.0 0.7 gather_fusion.1
  27.6 0.1 copy.30
  27.7 0.1 gt.22
  27.8 0.7 gather_fusion
  28.5 2.8 %gather_fusion.5 = bf16[16,256,512]{2,1,0:T(8,128)(2,1)} fusion(bf16[8,256,512]{2,1,0:T(8,128)(2,1)S(1)} %copy-done, s32[1024]{0:T(1024)S(1)} %pad_clamp_fusion.2), kind=kCustom, calls=%fused_computation.5 | custom fusion | bytes 8388672 | tf_op jit(solution)/shard_map/gather | solution.py:102
  31.3 2.0 gather_fusion.8
  33.4 3.3 %gather_fusion.3 = bf16[16,256,256]{2,1,0:T(8,128)(2,1)} fusion(bf16[8,256,256]{2,1,0:T(8,128)(2,1)} %param.20, s32[1024]{0:T(1024)S(1)} %pad_clamp_fusion.3), kind=kCustom, calls=%fused_computation.3 | custom fusion | bytes 4194368 | tf_op jit(solution)/shard_map/gather | solution.py:104
  36.7 33.9 %all-to-all-done = bf16[8,2,512,256]{3,2,1,0:T(8,128)(2,1)} async-done(((bf16[8,2,512,256]{3,2,1,0:T(8,128)(2,1)}), bf16[8,2,512,256]{3,2,1,0:T(8,128)(2,1)}, u32[]{:S(2)}, u32[]{:S(2)}) %all-to-all-start) | async-done | bytes 4194336 | tf_op jit(solution)/shard_map/all_to_all | solution.py:92
  70.6 7.3 %fusion.8 = bf16[16,256,256]{2,1,0:T(8,128)(2,1)} fusion(bf16[16,256,256]{2,1,0:T(8,128)(2,1)} %gather_fusion.8, bf16[16,256,512]{2,1,0:T(8,128)(2,1)} %gather_fusion.5, bf16[16,512,256]{2,1,0:T(8,128)(2,1)} %bitcast.14), kind=kOutput, calls=%fused_computation.17 | convolution fusion | flops 1611661312 | bytes 12582912 | tf_op jit(solution)/shard_map/ntw,nuw->ntu/dot_general | solution.py:29
  77.8 5.4 %fusion.12 = bf16[16,256,256]{2,1,0:T(8,128)(2,1)} fusion(bf16[16,256,256]{2,1,0:T(8,128)(2,1)} %gather_fusion.3, bf16[16,256,256]{2,1,0:T(8,128)(2,1)} %fusion.8), kind=kOutput, calls=%fused_computation.20 | convolution fusion | flops 1075838976 | bytes 6291456 | tf_op jit(solution)/shard_map/nsu,nvu->nsv/dot_general | solution.py:35
  83.3 4.9 %fusion = f32[4,4,256,256]{3,1,2,0:T(4,128)S(1)} fusion(f32[16]{0:T(128)S(1)} %broadcast_select_fusion.1, s32[4,4]{1,0:T(4,128)S(1)} %multiply_add_fusion.1, s32[16]{0:T(128)S(1)} %gather_fusion, bf16[2,8,256,256]{3,2,1,0:T(8,128)(2,1)} %bitcast.81), kind=kOutput, calls=%fused_computation.11 | convolution fusion | flops 201327104 | bytes 6291648 | tf_op jit(solution)/shard_map/sb,bx->sx/dot_general | solution.py:109
  88.2 2.9 %copy.36 = f32[128,8,4,256]{3,1,2,0:T(8,128)} copy(f32[128,8,4,256]{3,2,1,0:T(4,128)S(1)} %bitcast.80) | data formatting | bytes 8388608
  91.1 0.1 select_reduce_fusion.1
  91.2 0.1 reshape.331
  91.3 10.8 %psum.7 = f32[4,4]{1,0:T(4,128)S(1)} all-reduce(f32[4,4]{1,0:T(4,128)S(1)} %reshape.331), channel_id=1, replica_groups=mesh['visit'=4,'patch'=8] {'visit'}, use_global_device_ids=true, to_apply=%region_10.11 | all-reduce | flops 16 | bytes 128 | tf_op jit(solution)/shard_map/psum | solution.py:118
  102.2 0.1 select_reduce_fusion
  102.3 0.1 copy.32
  102.4 0.3 broadcast_in_dim.91
  102.8 0.2 copy.37
  103.0 68.2 %reduce-scatter.2.cloned.1.call-done = f32[256,1024]{1,0:T(8,128)} async-done(((f32[1024,1024]{1,0:T(8,128)}), f32[256,1024]{1,0:T(8,128)}) %reduce-scatter.2.cloned.1.call-update) | async-done | bytes 1048592 | tf_op jit(solution)/shard_map/reduce_scatter | solution.py:117
  171.2 1.4 div.48
  172.6 3.2 %collective-permute-start = (f32[4,1024]{1,0:T(4,128)S(1)}, f32[4,1024]{1,0:T(4,128)S(1)}, u32[]{:S(2)}, u32[]{:S(2)}) collective-permute-start(f32[4,1024]{1,0:T(4,128)S(1)} %get-tuple-element.8), channel_id=1, source_target_pairs={{0,8},{8,16},{16,24},{1,9},{9,17},{17,25},{2,10},{10,18},{18,26},{... | collective-permute-start | bytes 49160 | tf_op jit(solution)/shard_map/ppermute | solution.py:17
  175.8 1.3 collective-permute-start.1
  177.1 3.5 %collective-permute-done.1 = f32[4,1024]{1,0:T(4,128)S(1)} collective-permute-done((f32[4,1024]{1,0:T(4,128)S(1)}, f32[4,1024]{1,0:T(4,128)S(1)}, u32[]{:S(2)}, u32[]{:S(2)}) %collective-permute-start.1) | collective-permute-done | bytes 16416 | tf_op jit(solution)/shard_map/ppermute | solution.py:20
  180.6 0.1 pad_maximum_fusion
  180.7 0.1 fusion.55
  180.8 4.8 %collective-permute-start.2 = (f32[264,4]{1,0:T(8,128)S(1)}, f32[264,4]{1,0:T(8,128)S(1)}, u32[]{:S(2)}, u32[]{:S(2)}) collective-permute-start(f32[264,4]{1,0:T(8,128)S(1)} %get-tuple-element.7), channel_id=1, source_target_pairs={{0,1},{1,2},{2,3},{3,4},{4,5},{5,6},{6,7},{8,9},{9,10},{10,11},{11... | collective-permute-start | bytes 12680 | tf_op jit(solution)/shard_map/ppermute | solution.py:17
  185.6 2.1 collective-permute-start.3
  187.7 0.7 fusion.57
  188.5 3.6 %collective-permute-done.3 = f32[264,4]{1,0:T(8,128)} collective-permute-done((f32[264,4]{1,0:T(8,128)S(1)}, f32[264,4]{1,0:T(8,128)}, u32[]{:S(2)}, u32[]{:S(2)}) %collective-permute-start.3) | collective-permute-done | bytes 4256 | tf_op jit(solution)/shard_map/ppermute | solution.py:20
  192.1 1.7 concatenate.7
  193.8 6.8 %fusion.17 = f32[256,1032]{1,0:T(8,128)S(1)} fusion(f32[264,1032]{1,0:T(8,128)S(1)} %concatenate.7, f32[]{:T(128)} %bitcast.28, f32[]{:T(128)} %bitcast.27, f32[]{:T(128)} %bitcast.26, f32[]{:T(128)} %bitcast.25, f32[]{:T(128)} %bitcast.24, f32[]{:T(128)} %bitcast.23, f32[]{:T(128)} %bitcast.22, f32[]{:T(128)} %bitcast.21, f32[]{:T(128)} %bitcast.20), kind=kLoop, calls=%fused_computation.22 | loop fusion | flops 4491264 | bytes 10567716 | tf_op jit(solution)/shard_map/add | solution.py:131
  200.6 8.8 %fusion.26 = f32[256,1024]{1,0:T(8,128)} fusion(f32[256,1032]{1,0:T(8,128)S(1)} %fusion.17, f32[]{:T(128)} %bitcast.28, f32[]{:T(128)} %bitcast.27, f32[]{:T(128)} %bitcast.26, f32[]{:T(128)} %bitcast.25, f32[]{:T(128)} %bitcast.24, f32[]{:T(128)} %bitcast.23, f32[]{:T(128)} %bitcast.22, f32[]{:T(128)} %bitcast.21, f32[]{:T(128)} %bitcast.20), kind=kLoop, calls=%fused_computation.42 | loop fusion | flops 4456448 | bytes 10485796 | tf_op jit(solution)/shard_map/add | solution.py:134
  (52 shorter events, 0.6 us)
Async XLA Ops:
  7.2 21.4 %copy-start = (bf16[8,256,512]{2,1,0:T(8,128)(2,1)S(1)}, bf16[8,256,512]{2,1,0:T(8,128)(2,1)}, u32[]{:S(2)}) copy-start(bf16[8,256,512]{2,1,0:T(8,128)(2,1)} %param.18) | copy-start | bytes 6291460
  19.5 5.4 %copy-start.3 = (s32[512]{0:T(512)S(1)}, s32[512]{0:T(512)}, u32[]{:S(2)}) copy-start(s32[512]{0:T(512)} %param.16) | copy-start | bytes 6148
  19.5 6.1 %copy-start.4 = (s32[512]{0:T(512)S(1)}, s32[512]{0:T(512)}, u32[]{:S(2)}) copy-start(s32[512]{0:T(512)} %param.17) | copy-start | bytes 6148
  19.5 6.7 %copy-start.1 = (s32[128]{0:T(128)S(1)}, s32[128]{0:T(128)}, u32[]{:S(2)}) copy-start(s32[128]{0:T(128)} %param.13) | copy-start | bytes 1540
  19.5 7.4 %copy-start.2 = (f32[128]{0:T(128)S(1)}, f32[128]{0:T(128)}, u32[]{:S(2)}) copy-start(f32[128]{0:T(128)} %param.12) | copy-start | bytes 1540
  19.6 51.0 %all-to-all-start = ((bf16[8,2,512,256]{3,2,1,0:T(8,128)(2,1)}), bf16[8,2,512,256]{3,2,1,0:T(8,128)(2,1)}, u32[]{:S(2)}, u32[]{:S(2)}) async-start(bf16[8,2,512,256]{3,2,1,0:T(8,128)(2,1)} %broadcast_select_fusion), calls=%async_computation | async-start | bytes 8388608 | tf_op jit(solution)/shard_map/all_to_all | solution.py:92
  24.9 2.9 %copy-start.5 = (s32[512]{0:T(512)S(1)}, s32[512]{0:T(512)}, u32[]{:S(2)}) copy-start(s32[512]{0:T(512)} %param.15) | copy-start | bytes 6148
  24.9 146.2 %reduce-scatter.2.cloned.1.call-start = ((), (), s32[]{:S(2)}) async-start(), calls=%async_computation.2 | async-start | bytes 5242880 | tf_op jit(solution)/shard_map/reduce_scatter | solution.py:117
  28.5 2.8 %copy-start.8 = (bf16[8,256,256]{2,1,0:T(8,128)(2,1)S(1)}, bf16[8,256,256]{2,1,0:T(8,128)(2,1)}, u32[]{:S(2)}) copy-start(bf16[8,256,256]{2,1,0:T(8,128)(2,1)} %param.19) | copy-start | bytes 3145732
  172.6 15.9 %copy-start.7 = (f32[256,1024]{1,0:T(8,128)}, f32[256,1024]{1,0:T(8,128)S(1)}, u32[]{:S(2)}) copy-start(f32[256,1024]{1,0:T(8,128)S(1)} %div.48) | copy-start | bytes 3145732
  172.6 15.2 %copy-start.9 = (f32[9]{0:T(128)S(1)}, f32[9]{0:T(128)}, u32[]{:S(2)}) copy-start(f32[9]{0:T(128)} %param.21) | copy-start | bytes 112
  172.6 4.5 %collective-permute-start = (f32[4,1024]{1,0:T(4,128)S(1)}, f32[4,1024]{1,0:T(4,128)S(1)}, u32[]{:S(2)}, u32[]{:S(2)}) collective-permute-start(f32[4,1024]{1,0:T(4,128)S(1)} %get-tuple-element.8), channel_id=1, source_target_pairs={{0,8},{8,16},{16,24},{1,9},{9,17},{17,25},{2,10},{10,18},{18,26},{... | collective-permute-start | bytes 49160 | tf_op jit(solution)/shard_map/ppermute | solution.py:17
  175.8 4.8 %collective-permute-start.1 = (f32[4,1024]{1,0:T(4,128)S(1)}, f32[4,1024]{1,0:T(4,128)S(1)}, u32[]{:S(2)}, u32[]{:S(2)}) collective-permute-start(f32[4,1024]{1,0:T(4,128)S(1)} %get-tuple-element.9), channel_id=1, source_target_pairs={{8,0},{16,8},{24,16},{9,1},{17,9},{25,17},{10,2},{18,10},{26,18},{... | collective-permute-start | bytes 49160 | tf_op jit(solution)/shard_map/ppermute | solution.py:20
  180.7 7.7 %copy-start.6 = (f32[264,1024]{1,0:T(8,128)}, f32[264,1024]{1,0:T(8,128)S(1)}, u32[]{:S(2)}) copy-start(f32[264,1024]{1,0:T(8,128)S(1)} %pad_maximum_fusion) | copy-start | bytes 3244036
  180.8 7.6 %collective-permute-start.2 = (f32[264,4]{1,0:T(8,128)S(1)}, f32[264,4]{1,0:T(8,128)S(1)}, u32[]{:S(2)}, u32[]{:S(2)}) collective-permute-start(f32[264,4]{1,0:T(8,128)S(1)} %get-tuple-element.7), channel_id=1, source_target_pairs={{0,1},{1,2},{2,3},{3,4},{4,5},{5,6},{6,7},{8,9},{9,10},{10,11},{11... | collective-permute-start | bytes 12680 | tf_op jit(solution)/shard_map/ppermute | solution.py:17
  185.6 6.4 %collective-permute-start.3 = (f32[264,4]{1,0:T(8,128)S(1)}, f32[264,4]{1,0:T(8,128)}, u32[]{:S(2)}, u32[]{:S(2)}) collective-permute-start(f32[264,4]{1,0:T(8,128)S(1)} %get-tuple-element.6), channel_id=1, source_target_pairs={{1,0},{2,1},{3,2},{4,3},{5,4},{6,5},{7,6},{9,8},{10,9},{11,10},{12... | collective-permute-start | bytes 12680 | tf_op jit(solution)/shard_map/ppermute | solution.py:20
Sparse Core Ops, SparseCore 0:
  91.2 79.8 reduce-scatter.1
where the time goes:
time: 217 us; the launch traced here: 216 us
  waiting for transfers between devices  109 us (50%)
  local copies, waits for them, and re-layouts  23.8 us (11%)
  other arithmetic  23.8 us (11%)
  matrix products  17.6 us (8%)
  starting transfers between devices  16.8 us (8%)
  between operations  14.3 us (7%)
  blocking collectives  10.8 us (5%)
    reduce_scatter x1, waiting for transfers between devices, body(): lax.psum_scatter(partial_value, 'visit', scatter_dimension=0, tiled=True)  68.2 us
    all_to_all x1, waiting for transfers between devices, body(): lax.all_to_all(outgoing.reshape(n_patch, CAP, ccd_images.shape[1], ccd_im...  33.9 us
    psum x1, blocking collectives, body(): totals = lax.psum(tile_weights, 'visit')  10.8 us
    add x1, other arithmetic, body(): detection + detect_kernel[offset] * row_pass[:, offset:offset + width]  8.84 us
    ppermute x2, starting transfers between devices, extended(): lax.ppermute(lax.slice_in_dim(block, block.shape[dim] - width, None, axis...  8.01 us
    dot_general x1, matrix products, warp_entries(): jnp.einsum('ntw,nuw->ntu', first, col_tables, preferred_element_type=jnp....  7.26 us
    ppermute x2, waiting for transfers between devices, extended(): lax.ppermute(lax.slice_in_dim(block, 0, width, axis=dim), axis, backward)  7.08 us
    add x1, other arithmetic, body(): row_pass + detect_kernel[offset] * padded[offset:offset + height, :]  6.82 us
  transfers between devices with their start and end apart: 6, of which 4 were waited for; matrix products, arithmetic and copies ran while one was open for 6% of the time, Pallas kernels for 0%

commit v1 on v0

v1 whole, which is shorter than its diff:
```python
import functools

import jax
import jax.numpy as jnp
from jax import lax
from jax.experimental import pallas as pl
from jax.experimental.pallas import tpu as pltpu
from jax.sharding import PartitionSpec as P

K_OV = 4
TS = 256
G = 4
CAP = 2
STEPS = 4
BAND = 16
EDGE_R = 8
EDGE_C = 128
MESH = pl.DeviceIdType.MESH
F32 = jnp.float32
BF16 = jnp.bfloat16
NT = (((1,), (1,)), ((), ()))


def kernel(
    n_visit,
    n_patch,
    images,
    row_tables,
    col_tables,
    psf_tables,
    taps,
    weight,
    psf_index,
    target,
    slot,
    row_pick,
    col_pick,
    target_v,
    slot_v,
    weight_v,
    coadd,
    detection,
    second,
    psf_of,
    outbox,
    inbox,
    sums,
    arrived,
    mix_hi,
    mix_lo,
    ext,
    p_send,
    p_recv,
    v_send,
    v_recv,
    h_send,
    h_recv,
):
    v = lax.axis_index("visit")
    p = lax.axis_index("patch")
    per_device = images.shape[0] * K_OV
    boxes = n_patch * CAP
    rows = coadd.shape[0]
    width = coadd.shape[1]
    step_rows = rows // STEPS
    parts = TS // rows
    base = (v * n_patch + p) * per_device

    def entry_for(start, patch, rank):
        seen = jnp.int32(0)
        found = jnp.int32(0)
        filled = jnp.int32(0)
        for e in range(per_device):
            hit = target[start + e] == patch
            take = jnp.logical_and(hit, seen == rank)
            found = jnp.where(take, e, found)
            filled = jnp.where(take, 1, filled)
            seen = seen + hit.astype(jnp.int32)
        return found, filled

    ext[...] = jnp.zeros_like(ext)
    barrier = pltpu.get_barrier_semaphore()
    for d in range(1, n_patch):
        pl.semaphore_signal(
            barrier, inc=1, device_id=(v, lax.rem(p + d, n_patch)), device_id_type=MESH
        )
    for d in range(1, n_visit):
        pl.semaphore_signal(
            barrier, inc=1, device_id=(lax.rem(v + d, n_visit), p), device_id_type=MESH
        )
    corners = [(dv, dp) for dv in (-1, 1) for dp in (-1, 1)]
    sides = [(-1, 0), (1, 0), (0, -1), (0, 1)]

    def inside(dv, dp):
        ok = None
        for at, shift, count in ((v, dv, n_visit), (p, dp, n_patch)):
            if shift < 0:
                term = at > 0
            elif shift > 0:
                term = at < count - 1
            else:
                continue
            ok = term if ok is None else jnp.logical_and(ok, term)
        return ok

    for dv, dp in corners:
        there = (lax.rem(v + dv + n_visit, n_visit), lax.rem(p + dp + n_patch, n_patch))
        pl.semaphore_signal(barrier, inc=1, device_id=there, device_id_type=MESH)

    def warp(s, _):
        entry, _filled = entry_for(base, s // CAP, lax.rem(s, CAP))
        image = images[entry // K_OV]
        first = jnp.dot(
            row_tables[row_pick[base + entry]], image, preferred_element_type=F32
        ).astype(BF16)
        second[s] = lax.dot_general(
            first, col_tables[col_pick[base + entry]], NT, preferred_element_type=F32
        ).astype(BF16)
        psf_of[s] = psf_index[(base + entry) // K_OV]
        return 0

    lax.fori_loop(0, boxes, warp, 0)

    def match(c):
        def one(s, _):
            table = psf_tables[psf_of[s]]
            for h in range(parts):
                at = pl.multiple_of(h * rows + c * step_rows, step_rows)
                left = psf_tables[psf_of[s], pl.ds(at, step_rows), :]
                third = jnp.dot(left, second[s], preferred_element_type=F32).astype(BF16)
                outbox[c, s, h * step_rows : (h + 1) * step_rows, :] = lax.dot_general(
                    third, table, NT, preferred_element_type=F32
                ).astype(BF16)
            return 0

        lax.fori_loop(0, boxes, one, 0)

    def patch_copy(c, d):
        there = lax.rem(p + d, n_patch)
        return pltpu.make_async_remote_copy(
            src_ref=outbox.at[c, pl.ds(there * CAP, CAP)],
            dst_ref=inbox.at[c, pl.ds(p * CAP, CAP)],
            send_sem=p_send.at[c, d - 1],
            recv_sem=p_recv.at[c, d - 1],
            device_id=(v, there),
            device_id_type=MESH,
        )

    def visit_copy(c, d):
        there = lax.rem(v + d, n_visit)
        return pltpu.make_async_remote_copy(
            src_ref=sums.at[c, there],
            dst_ref=arrived.at[c, d - 1],
            send_sem=v_send.at[c, d - 1],
            recv_sem=v_recv.at[c, d - 1],
            device_id=(there, p),
            device_id_type=MESH,
        )

    def send_patch(c):
        for d in range(1, n_patch):
            patch_copy(c, d).start()
        inbox[c, pl.ds(p * CAP, CAP)] = outbox[c, pl.ds(p * CAP, CAP)]

    def combine(c):
        for d in range(1, n_patch):
            patch_copy(c, d).wait_recv()
        for h in range(parts):

            def band(i, _):
                at = pl.multiple_of(h * step_rows + i * BAND, BAND)
                tiles = inbox[c, :, pl.ds(at, BAND), :].reshape(boxes * BAND, TS)
                total = jnp.dot(
                    mix_hi[...].reshape(G * G * BAND, boxes * BAND),
                    tiles,
                    preferred_element_type=F32,
                )
                total = total + jnp.dot(
                    mix_lo[...].reshape(G * G * BAND, boxes * BAND),
                    tiles,
                    preferred_element_type=F32,
                )
                total = total.astype(BF16).reshape(G, G, BAND, TS)
                to = pl.multiple_of(i * BAND, BAND)
                for g in range(G):
                    sums[c, g * parts + h, :, pl.ds(to, BAND), :] = total[g]
                return 0

            lax.fori_loop(0, step_rows // BAND, band, 0)
        for d in range(1, n_visit):
            visit_copy(c, d).start()

    match(0)
    pl.semaphore_wait(barrier, n_patch - 1 + n_visit - 1 + len(corners))
    send_patch(0)

    lanes = lax.broadcasted_iota(jnp.int32, (BAND, boxes * BAND), 1)
    sublanes = lax.broadcasted_iota(jnp.int32, (BAND, boxes * BAND), 0)
    diagonal = lax.rem(lanes, BAND) == sublanes
    lane_box = lanes // BAND

    def gather(b, carry):
        slots, weights = carry
        start = (v * n_patch + b // CAP) * per_device
        entry, filled = entry_for(start, p, lax.rem(b, CAP))
        value = jnp.where(filled > 0, weight[(start + entry) // K_OV], 0.0)
        here = lane_box == b
        return (
            jnp.where(here, slot[start + entry], slots),
            jnp.where(here, value, weights),
        )

    slots, weights = lax.fori_loop(
        0,
        boxes,
        gather,
        (jnp.zeros(lanes.shape, jnp.int32), jnp.zeros(lanes.shape, F32)),
    )

    def mix(s, _):
        full = jnp.where(jnp.logical_and(slots == s, diagonal), weights, 0.0)
        high = full.astype(BF16)
        mix_hi[s] = high
        mix_lo[s] = (full - high.astype(F32)).astype(BF16)
        return 0

    lax.fori_loop(0, G * G, mix, 0)

    def step(c, _):
        match(c + 1)
        send_patch(c + 1)
        combine(c)
        return 0

    lax.fori_loop(0, STEPS - 1, step, 0)
    combine(STEPS - 1)

    tile_row = (v * rows) // TS
    scales = []
    for g in range(G):
        chosen = jnp.logical_and(target_v[...] == p, slot_v[...] == tile_row * G + g)
        scales.append(1.0 + jnp.sum(jnp.where(chosen, weight_v[...], 0.0)))

    def finish(c, _):
        for d in range(1, n_visit):
            visit_copy(c, d).wait_recv()
        for g in range(G):
            total = sums[c, v, g].astype(F32)
            for d in range(1, n_visit):
                total = total + arrived[c, d - 1, g].astype(F32)
            value = total / scales[g]
            at = pl.multiple_of(c * step_rows, step_rows)
            coadd[pl.ds(at, step_rows), g * TS : (g + 1) * TS] = value
            ext[pl.ds(EDGE_R + at, step_rows), EDGE_C + g * TS : EDGE_C + (g + 1) * TS] = value
        return 0

    lax.fori_loop(0, STEPS, finish, 0)

    def span(shift, edge, length):
        if shift < 0:
            return pl.ds(edge, edge), pl.ds(edge + length, edge)
        if shift > 0:
            return pl.ds(length, edge), pl.ds(0, edge)
        return pl.ds(edge, length), pl.ds(edge, length)

    def border(k, dv, dp):
        r_from, r_to = span(dv, EDGE_R, rows)
        c_from, c_to = span(dp, EDGE_C, width)
        return pltpu.make_async_remote_copy(
            src_ref=ext.at[r_from, c_from],
            dst_ref=ext.at[r_to, c_to],
            send_sem=h_send.at[k],
            recv_sem=h_recv.at[k],
            device_id=(v + dv, p + dp),
            device_id_type=MESH,
        )

    around = sides + corners
    for k, (dv, dp) in enumerate(around):

        @pl.when(inside(dv, dp))
        def _():
            border(k, dv, dp).start()

    for k, (dv, dp) in enumerate(around):

        @pl.when(inside(-dv, -dp))
        def _():
            border(k, dv, dp).wait_recv()

    count = taps.shape[0]
    radius = count // 2
    block = 16

    def filtered(i, _):
        at = pl.multiple_of(i * block, block)
        held = ext[pl.ds(at, block + 2 * EDGE_R), :]
        low = EDGE_R - radius
        across = taps[0] * held[low : low + block, :]
        for j in range(1, count):
            across = across + taps[j] * held[low + j : low + j + block, :]
        low = EDGE_C - radius
        result = taps[0] * across[:, low : low + width]
        for j in range(1, count):
            result = result + taps[j] * across[:, low + j : low + j + width]
        detection[pl.ds(at, block), :] = result
        return 0

    lax.fori_loop(0, rows // block, filtered, 0)

    for k, (dv, dp) in enumerate(around):

        @pl.when(inside(dv, dp))
        def _():
            border(k, dv, dp).wait_send()

    def drain(c, _):
        for d in range(1, n_patch):
            patch_copy(c, d).wait_send()
        for d in range(1, n_visit):
            visit_copy(c, d).wait_send()
        return 0

    lax.fori_loop(0, STEPS, drain, 0)


def body(
    ccd_images,
    ccd_weight,
    psf_index,
    patch_target,
    tile_slot,
    row_matrix,
    col_matrix,
    warp_rows,
    warp_cols,
    psf_match,
    detect_kernel,
):
    n_visit = lax.axis_size("visit")
    n_patch = lax.axis_size("patch")
    rows = G * TS // n_visit
    width = G * TS
    step_rows = rows // STEPS
    high = TS // rows * step_rows
    boxes = n_patch * CAP
    targets = patch_target[:, 0]
    entries = targets.shape[0]
    vector = (entries // 128, 128)
    smem = pl.BlockSpec(memory_space=pltpu.SMEM)
    vmem = pl.BlockSpec(memory_space=pltpu.VMEM)
    out = jax.ShapeDtypeStruct((rows, width), F32)
    return pl.pallas_call(
        functools.partial(kernel, n_visit, n_patch),
        out_shape=(out, out),
        in_specs=[vmem] * 4 + [smem] * 7 + [vmem] * 3,
        out_specs=(vmem, vmem),
        scratch_shapes=[
            pltpu.VMEM((boxes, TS, TS), BF16),
            pltpu.SMEM((boxes,), jnp.int32),
            pltpu.VMEM((STEPS, boxes, high, TS), BF16),
            pltpu.VMEM((STEPS, boxes, high, TS), BF16),
            pltpu.VMEM((STEPS, n_visit, G, step_rows, TS), BF16),
            pltpu.VMEM((STEPS, n_visit - 1, G, step_rows, TS), BF16),
            pltpu.VMEM((G * G, BAND, boxes * BAND), BF16),
            pltpu.VMEM((G * G, BAND, boxes * BAND), BF16),
            pltpu.VMEM((rows + 2 * EDGE_R, width + 2 * EDGE_C), F32),
            pltpu.SemaphoreType.DMA((STEPS, n_patch - 1)),
            pltpu.SemaphoreType.DMA((STEPS, n_patch - 1)),
            pltpu.SemaphoreType.DMA((STEPS, n_visit - 1)),
            pltpu.SemaphoreType.DMA((STEPS, n_visit - 1)),
            pltpu.SemaphoreType.DMA((8,)),
            pltpu.SemaphoreType.DMA((8,)),
        ],
        compiler_params=pltpu.CompilerParams(
            collective_id=0, has_side_effects=True, vmem_limit_bytes=48 * 1024 * 1024
        ),
    )(
        ccd_images,
        warp_rows,
        warp_cols,
        psf_match,
        detect_kernel,
        ccd_weight,
        psf_index,
        targets,
        tile_slot,
        row_matrix,
        col_matrix,
        targets.reshape(vector),
        tile_slot.reshape(vector),
        jnp.repeat(ccd_weight, K_OV).reshape(vector),
    )


def solution(mesh):
    in_specs = (P(("visit", "patch"), None, None), P(), P(), P(), P(), P(), P(), P(), P(), P(), P())
    out_specs = (P("visit", "patch"), P("visit", "patch"))
    return jax.shard_map(body, mesh=mesh, in_specs=in_specs, out_specs=out_specs, check_vma=False)
```

time: 217 us -> 95.8 us (0.44)
  waiting for transfers between devices: 109 us -> 0 us
  Pallas kernels: 0 us -> 83.3 us
  other arithmetic: 23.8 us -> 0 us
  matrix products: 17.6 us -> 0 us
  starting transfers between devices: 16.8 us -> 0 us
  between operations: 14.3 us -> 0.66 us
  local copies, waits for them, and re-layouts: 23.8 us -> 11.2 us
  blocking collectives: 10.8 us -> 0 us
    pallas_call x0 -> x1, Pallas kernels: none -> 83.3 us  [body(): pl.pallas_call(functools.partial(kernel, n_visit, n_patch), out_shape=(ou...]
    reduce_scatter x1 -> x0, waiting for transfers between devices: 68.2 us -> none  [body(): lax.psum_scatter(partial_value, 'visit', scatter_dimension=0, tiled=True)]
    all_to_all x1 -> x0, waiting for transfers between devices: 33.9 us -> none  [body(): lax.all_to_all(outgoing.reshape(n_patch, CAP, ccd_images.shape[1], ccd_im...]
    dot_general x3 -> x0, matrix products: 17.6 us -> none  [the longest x1 7.26 us: warp_entries(): jnp.einsum('ntw,nuw->ntu', first, col_tables, preferred_element_type=jnp....]
    add x7 -> x0, other arithmetic: 15.7 us -> none  [the longest x1 8.84 us: body(): detection + detect_kernel[offset] * row_pass[:, offset:offset + width]]
    gather x9 -> x0, local copies, waits for them, and re-layouts: 15.4 us -> none  [the longest x1 3.97 us: body(): ccd_images[sender_entry // K_OV]]
    ppermute x4 -> x0, starting transfers between devices: 11.4 us -> none  [the longest x2 8.01 us: extended(): lax.ppermute(lax.slice_in_dim(block, block.shape[dim] - width, None, axis...]
    psum x1 -> x0, blocking collectives: 10.8 us -> none  [body(): totals = lax.psum(tile_weights, 'visit')]
  transfers between devices with their start and end apart: 6 -> 0, of which waited for: 4 -> 0; matrix products, arithmetic and copies ran while one was open for 6% -> 0% of each run, Pallas kernels for 0% -> 0%
where the time goes in v1:
time: 95.8 us; the launch traced here: 95.2 us
  Pallas kernels  83.3 us (87%)
  local copies, waits for them, and re-layouts  11.2 us (12%)
    pallas_call x1, Pallas kernels, body(): pl.pallas_call(functools.partial(kernel, n_visit, n_patch), out_shape=(ou...  83.3 us
    unnamed x22, local copies, waits for them, and re-layouts  10.3 us

profile of v1, /device:TPU:1, one launch (start us, length us, event | category | flops | bytes accessed | tf_op | source)
XLA Modules:
  0.0 95.2 jit_solution(3731317382955194665)
XLA Ops:
  0.6 0.7 broadcast_in_dim.7
  1.4 0.1 broadcast_in_dim.8
  1.4 0.1 broadcast_in_dim.9.weight_v
  1.6 0.0 copy-start
  1.6 1.2 %copy-done = bf16[4,512,256]{2,1,0:T(8,128)(2,1)S(1)} copy-done((bf16[4,512,256]{2,1,0:T(8,128)(2,1)S(1)}, bf16[4,512,256]{2,1,0:T(8,128)(2,1)}, u32[]{:S(2)}) %copy-start) | copy-done | bytes 1048600
  2.8 0.0 copy-start.1
  2.8 1.2 %copy-done.1 = bf16[8,256,256]{2,1,0:T(8,128)(2,1)S(1)} copy-done((bf16[8,256,256]{2,1,0:T(8,128)(2,1)S(1)}, bf16[8,256,256]{2,1,0:T(8,128)(2,1)}, u32[]{:S(2)}) %copy-start.1) | copy-done | bytes 1048600
  4.0 0.0 copy-start.2
  4.0 1.2 %copy-done.2 = bf16[8,256,256]{2,1,0:T(8,128)(2,1)S(1)} copy-done((bf16[8,256,256]{2,1,0:T(8,128)(2,1)S(1)}, bf16[8,256,256]{2,1,0:T(8,128)(2,1)}, u32[]{:S(2)}) %copy-start.2) | copy-done | bytes 1048600
  5.2 0.0 copy-start.3
  5.2 0.7 copy-done.3
  5.9 0.0 copy-start.4
  5.9 0.7 copy-done.4
  6.6 0.0 copy-start.5
  6.6 0.7 copy-done.5
  7.3 0.0 copy-start.6
  7.3 0.7 copy-done.6
  8.0 0.0 copy-start.7
  8.0 0.7 copy-done.7
  8.6 0.0 copy-start.8
  8.6 0.7 copy-done.8
  9.3 0.0 copy-start.9
  9.3 0.7 copy-done.9
  9.9 83.3 %shard_map.122 = (f32[256,1024]{1,0:T(8,128)S(1)}, f32[256,1024]{1,0:T(8,128)S(1)}) custom-call(bf16[4,512,256]{2,1,0:T(8,128)(2,1)S(1)} %copy-done, bf16[8,256,512]{2,1,0:T(8,128)(2,1)} %row_tables.1, bf16[8,256,256]{2,1,0:T(8,128)(2,1)S(1)} %copy-done.1, bf16[8,256,256]{2,1,0:T(8,128)(2,1)S(1)} %copy-done.2, f32[9]{0:T(128)S(1)} %copy-done.8, ...), custom_call_target="tpu_custom_call" | custom-call | tf_op jit(solution)/shard_map/pallas_call | solution.py:353
  93.3 1.0 %copy.15 = f32[256,1024]{1,0:T(8,128)} copy(f32[256,1024]{1,0:T(8,128)S(1)} %get-tuple-element.4) | data formatting | bytes 2097152
  94.2 1.0 %copy.16 = f32[256,1024]{1,0:T(8,128)} copy(f32[256,1024]{1,0:T(8,128)S(1)} %get-tuple-element.5) | data formatting | bytes 2097152
Async XLA Ops:
  1.6 1.2 %copy-start = (bf16[4,512,256]{2,1,0:T(8,128)(2,1)S(1)}, bf16[4,512,256]{2,1,0:T(8,128)(2,1)}, u32[]{:S(2)}) copy-start(bf16[4,512,256]{2,1,0:T(8,128)(2,1)} %images.1) | copy-start | bytes 3145732
  2.8 1.2 %copy-start.1 = (bf16[8,256,256]{2,1,0:T(8,128)(2,1)S(1)}, bf16[8,256,256]{2,1,0:T(8,128)(2,1)}, u32[]{:S(2)}) copy-start(bf16[8,256,256]{2,1,0:T(8,128)(2,1)} %col_tables.1) | copy-start | bytes 3145732
  4.0 1.2 %copy-start.2 = (bf16[8,256,256]{2,1,0:T(8,128)(2,1)S(1)}, bf16[8,256,256]{2,1,0:T(8,128)(2,1)}, u32[]{:S(2)}) copy-start(bf16[8,256,256]{2,1,0:T(8,128)(2,1)} %psf_tables.1) | copy-start | bytes 3145732
  5.2 0.7 copy-start.3
  5.9 0.7 copy-start.4
  6.6 0.7 copy-start.5
  7.3 0.7 copy-start.6
  8.0 0.7 copy-start.7
  8.6 0.7 copy-start.8
  9.3 0.7 copy-start.9

commit v2 on v1

v2 whole, which is shorter than its diff:
```python
import functools

import jax
import jax.numpy as jnp
from jax import lax
from jax.experimental import pallas as pl
from jax.experimental.pallas import tpu as pltpu
from jax.sharding import PartitionSpec as P

K_OV = 4
TS = 256
G = 4
CAP = 2
STEPS = 8
AHEAD = 2
BAND = 16
EDGE_R = 8
EDGE_C = 128
MESH = pl.DeviceIdType.MESH
F32 = jnp.float32
BF16 = jnp.bfloat16
NT = (((1,), (1,)), ((), ()))


def kernel(
    n_visit,
    n_patch,
    images_hbm,
    rows_hbm,
    cols_hbm,
    psf_hbm,
    taps,
    weight,
    psf_index,
    target,
    slot,
    row_pick,
    col_pick,
    coadd,
    detection,
    images,
    row_tables,
    col_tables,
    psf_tables,
    matched,
    entry_of,
    slot_weight,
    outbox,
    inbox,
    sums,
    arrived,
    mix,
    ext,
    load_sem,
    p_send,
    p_recv,
    v_send,
    v_recv,
    c_send,
    c_recv,
    r_send,
    r_recv,
):
    v = lax.axis_index("visit")
    p = lax.axis_index("patch")
    n_images = images.shape[0]
    per_device = n_images * K_OV
    boxes = n_patch * CAP
    rows = coadd.shape[0]
    width = coadd.shape[1]
    step_rows = rows // STEPS
    parts = TS // rows
    own = v * n_patch + p
    base = own * per_device

    loads = [
        pltpu.make_async_copy(rows_hbm, row_tables, load_sem.at[0]),
        pltpu.make_async_copy(images_hbm, images, load_sem.at[1]),
        pltpu.make_async_copy(cols_hbm, col_tables, load_sem.at[2]),
        pltpu.make_async_copy(psf_hbm, psf_tables, load_sem.at[3]),
    ]
    for load in loads:
        load.start()

    def entry_for(start, patch, rank):
        seen = jnp.int32(0)
        found = jnp.int32(0)
        filled = jnp.int32(0)
        for e in range(per_device):
            hit = target[start + e] == patch
            take = jnp.logical_and(hit, seen == rank)
            found = jnp.where(take, e, found)
            filled = jnp.where(take, 1, filled)
            seen = seen + hit.astype(jnp.int32)
        return found, filled

    ext[...] = jnp.zeros_like(ext)
    arrived[0, :, 0] = jnp.zeros_like(arrived[0, :, 0])
    arrived[1, :, n_visit - 1] = jnp.zeros_like(arrived[1, :, n_visit - 1])
    corners = [(-1, -1), (-1, 1), (1, -1), (1, 1)]
    barrier = pltpu.get_barrier_semaphore()
    for d in range(1, n_patch):
        pl.semaphore_signal(
            barrier, inc=1, device_id=(v, lax.rem(p + d, n_patch)), device_id_type=MESH
        )
    for d in (1, n_visit - 1):
        pl.semaphore_signal(
            barrier, inc=1, device_id=(lax.rem(v + d, n_visit), p), device_id_type=MESH
        )
    for dv, dp in corners:
        there = (lax.rem(v + dv + n_visit, n_visit), lax.rem(p + dp + n_patch, n_patch))
        pl.semaphore_signal(barrier, inc=1, device_id=there, device_id_type=MESH)

    def inside(dv, dp):
        ok = None
        for at, shift, count in ((v, dv, n_visit), (p, dp, n_patch)):
            if shift < 0:
                term = at > 0
            elif shift > 0:
                term = at < count - 1
            else:
                continue
            ok = term if ok is None else jnp.logical_and(ok, term)
        return ok

    def find(s, _):
        entry_of[s] = entry_for(base, s // CAP, lax.rem(s, CAP))[0]
        return 0

    lax.fori_loop(0, boxes, find, 0)
    for load in loads:
        load.wait()

    def warp(i, _):
        image = images[i]
        table = psf_tables[psf_index[own * n_images + i]]
        at = base + i * K_OV
        first = [
            jnp.dot(row_tables[row_pick[at + j]], image, preferred_element_type=F32).astype(BF16)
            for j in range(K_OV)
        ]
        second = [
            lax.dot_general(
                first[j], col_tables[col_pick[at + j]], NT, preferred_element_type=F32
            ).astype(BF16)
            for j in range(K_OV)
        ]
        third = [
            jnp.dot(table, second[j], preferred_element_type=F32).astype(BF16)
            for j in range(K_OV)
        ]
        for j in range(K_OV):
            matched[i * K_OV + j] = lax.dot_general(
                third[j], table, NT, preferred_element_type=F32
            ).astype(BF16)
        return 0

    lax.fori_loop(0, n_images, warp, 0)

    def patch_copy(c, d):
        there = lax.rem(p + d, n_patch)
        return pltpu.make_async_remote_copy(
            src_ref=outbox.at[c, pl.ds(there * CAP, CAP)],
            dst_ref=inbox.at[c, pl.ds(p * CAP, CAP)],
            send_sem=p_send.at[c, d - 1],
            recv_sem=p_recv.at[c, d - 1],
            device_id=(v, there),
            device_id_type=MESH,
        )

    def send_patch(c):
        def fill(s, _):
            for h in range(parts):
                at = pl.multiple_of(h * rows + c * step_rows, step_rows)
                outbox[c, s, h * step_rows : (h + 1) * step_rows, :] = matched[
                    entry_of[s], pl.ds(at, step_rows), :
                ]
            return 0

        lax.fori_loop(0, boxes, fill, 0)
        for d in range(1, n_patch):
            patch_copy(c, d).start()
        inbox[c, pl.ds(p * CAP, CAP)] = outbox[c, pl.ds(p * CAP, CAP)]

    def hop(c, r, up):
        way = 0 if up else 1
        return pltpu.make_async_remote_copy(
            src_ref=sums.at[c, r],
            dst_ref=arrived.at[way, c, r],
            send_sem=v_send.at[way, c, r],
            recv_sem=v_recv.at[way, c, r],
            device_id=(v + (1 if up else -1), p),
            device_id_type=MESH,
        )

    def pass_on(c, up, add):
        for r in reversed(range(1, n_visit)) if up else range(n_visit - 1):

            @pl.when(v < r if up else v > r)
            def _():
                if add:
                    hop(c, r, up).wait_recv()
                    came = arrived[0 if up else 1, c, r].astype(F32)
                    sums[c, r] = (sums[c, r].astype(F32) + came).astype(BF16)
                hop(c, r, up).start()

    def combine(c):
        for d in range(1, n_patch):
            patch_copy(c, d).wait_recv()
        weights = mix[...].reshape(G * G * BAND, boxes * BAND)
        for h in range(parts):
            for i in range(step_rows // BAND):
                at = h * step_rows + i * BAND
                tiles = inbox[c, :, at : at + BAND, :].reshape(boxes * BAND, TS)
                total = jnp.dot(weights, tiles, preferred_element_type=F32)
                total = total.astype(BF16).reshape(G, G, BAND, TS)
                for g in range(G):
                    sums[c, g * parts + h, :, i * BAND : (i + 1) * BAND, :] = total[g]

        @pl.when(v == 0)
        def _():
            pass_on(c, True, False)

        @pl.when(v == n_visit - 1)
        def _():
            pass_on(c, False, False)

    def forward(c):
        @pl.when(jnp.logical_and(v > 0, 2 * v < n_visit))
        def _():
            pass_on(c, True, True)
            pass_on(c, False, True)

        @pl.when(jnp.logical_and(v < n_visit - 1, 2 * v >= n_visit))
        def _():
            pass_on(c, False, True)
            pass_on(c, True, True)

    def column_copy(c, k):
        at = pl.multiple_of(EDGE_R + c * step_rows, 8)
        here, there = (EDGE_C, EDGE_C + width) if k == 0 else (width, 0)
        return pltpu.make_async_remote_copy(
            src_ref=ext.at[pl.ds(at, step_rows), pl.ds(here, EDGE_C)],
            dst_ref=ext.at[pl.ds(at, step_rows), pl.ds(there, EDGE_C)],
            send_sem=c_send.at[k, c],
            recv_sem=c_recv.at[k, c],
            device_id=(v, p + (-1 if k == 0 else 1)),
            device_id_type=MESH,
        )

    def span(shift, edge, length):
        if shift < 0:
            return pl.ds(edge, edge), pl.ds(edge + length, edge)
        if shift > 0:
            return pl.ds(length, edge), pl.ds(0, edge)
        return pl.ds(edge, length), pl.ds(edge, length)

    around = [(-1, 0), (1, 0)] + corners

    def row_copy(k):
        dv, dp = around[k]
        r_from, r_to = span(dv, EDGE_R, rows)
        c_from, c_to = span(dp, EDGE_C, width)
        return pltpu.make_async_remote_copy(
            src_ref=ext.at[r_from, c_from],
            dst_ref=ext.at[r_to, c_to],
            send_sem=r_send.at[k],
            recv_sem=r_recv.at[k],
            device_id=(v + dv, p + dp),
            device_id_type=MESH,
        )

    def finish(c):
        @pl.when(v > 0)
        def _():
            hop(c, v, True).wait_recv()

        @pl.when(v < n_visit - 1)
        def _():
            hop(c, v, False).wait_recv()

        at = pl.multiple_of(c * step_rows, step_rows)
        for g in range(G):
            total = sums[c, v, g].astype(F32)
            total = total + arrived[0, c, v, g].astype(F32)
            total = total + arrived[1, c, v, g].astype(F32)
            value = total * (1.0 / (1.0 + jnp.full((1, TS), slot_weight[g])))
            coadd[pl.ds(at, step_rows), g * TS : (g + 1) * TS] = value
            ext[pl.ds(EDGE_R + at, step_rows), EDGE_C + g * TS : EDGE_C + (g + 1) * TS] = value
        for k in range(2):

            @pl.when(inside(0, -1 if k == 0 else 1))
            def _():
                column_copy(c, k).start()

        for k, (dv, dp) in enumerate(around):

            @pl.when(jnp.logical_and(c == (0 if dv < 0 else STEPS - 1), inside(dv, dp)))
            def _():
                row_copy(k).start()

    def columns_in(c):
        for k in range(2):

            @pl.when(inside(0, 1 if k == 0 else -1))
            def _():
                column_copy(c, k).wait_recv()

    count = taps.shape[0]
    radius = count // 2

    def detect(c):
        def one(i, _):
            at = pl.multiple_of(c * step_rows + i * BAND, BAND)
            held = ext[pl.ds(at, BAND + 2 * EDGE_R), :]
            low = EDGE_R - radius
            across = taps[0] * held[low : low + BAND, :]
            for j in range(1, count):
                across = across + taps[j] * held[low + j : low + j + BAND, :]
            low = EDGE_C - radius
            result = taps[0] * across[:, low : low + width]
            for j in range(1, count):
                result = result + taps[j] * across[:, low + j : low + j + width]
            detection[pl.ds(at, BAND), :] = result
            return 0

        lax.fori_loop(0, step_rows // BAND, one, 0)

    pl.semaphore_wait(barrier, n_patch - 1 + 2 + len(corners))
    for c in range(AHEAD):
        send_patch(c)

    lanes = lax.broadcasted_iota(jnp.int32, (BAND, boxes * BAND), 1)
    sublanes = lax.broadcasted_iota(jnp.int32, (BAND, boxes * BAND), 0)
    diagonal = lax.rem(lanes, BAND) == sublanes
    lane_box = lanes // BAND

    def gather(b, carry):
        slots, weights = carry
        start = (v * n_patch + b // CAP) * per_device
        entry, filled = entry_for(start, p, lax.rem(b, CAP))
        value = jnp.where(filled > 0, weight[(start + entry) // K_OV], 0.0)
        here = lane_box == b
        return (
            jnp.where(here, slot[start + entry], slots),
            jnp.where(here, value, weights),
        )

    slots, weights = lax.fori_loop(
        0,
        boxes,
        gather,
        (jnp.zeros(lanes.shape, jnp.int32), jnp.zeros(lanes.shape, F32)),
    )

    def place(s, _):
        full = jnp.where(jnp.logical_and(slots == s, diagonal), weights, 0.0)
        mix[s] = full.astype(BF16)
        return 0

    lax.fori_loop(0, G * G, place, 0)

    tile_row = (v * rows) // TS

    def tally(i, carry):
        carry = list(carry)
        for j in range(K_OV):
            e = i * K_OV + j
            mine = target[e] == p
            at = slot[e] - tile_row * G
            for g in range(G):
                chosen = jnp.logical_and(mine, at == g)
                carry[g] = carry[g] + jnp.where(chosen, weight[i], 0.0)
        return tuple(carry)

    totals = lax.fori_loop(0, weight.shape[0], tally, (jnp.float32(0),) * G)
    for g in range(G):
        slot_weight[g] = totals[g]

    def stage(t, first, last, do):
        @pl.when(jnp.logical_and(t >= first, t <= last))
        def _():
            do()

    def step(t, _):
        stage(t, 0, STEPS - 1 - AHEAD, lambda: send_patch(t + AHEAD))
        stage(t, 0, STEPS - 1, lambda: combine(t))
        stage(t, 1, STEPS, lambda: forward(t - 1))
        stage(t, 2, STEPS + 1, lambda: finish(t - 2))
        stage(t, 3, STEPS + 2, lambda: columns_in(t - 3))
        stage(t, 5, STEPS + 2, lambda: detect(t - 4))
        return 0

    lax.fori_loop(0, STEPS + 3, step, 0)
    for k, (dv, dp) in enumerate(around):

        @pl.when(inside(-dv, -dp))
        def _():
            row_copy(k).wait_recv()

    detect(STEPS - 1)
    detect(0)

    for k, (dv, dp) in enumerate(around):

        @pl.when(inside(dv, dp))
        def _():
            row_copy(k).wait_send()

    def drain(c, _):
        for d in range(1, n_patch):
            patch_copy(c, d).wait_send()
        for k in range(2):

            @pl.when(inside(0, -1 if k == 0 else 1))
            def _():
                column_copy(c, k).wait_send()

        for r in range(n_visit):

            @pl.when(jnp.logical_and(v < r, v < n_visit - 1))
            def _():
                hop(c, r, True).wait_send()

            @pl.when(jnp.logical_and(v > r, v > 0))
            def _():
                hop(c, r, False).wait_send()

        return 0

    lax.fori_loop(0, STEPS, drain, 0)


def body(
    ccd_images,
    ccd_weight,
    psf_index,
    patch_target,
    tile_slot,
    row_matrix,
    col_matrix,
    warp_rows,
    warp_cols,
    psf_match,
    detect_kernel,
):
    n_visit = lax.axis_size("visit")
    n_patch = lax.axis_size("patch")
    rows = G * TS // n_visit
    width = G * TS
    step_rows = rows // STEPS
    high = TS // rows * step_rows
    boxes = n_patch * CAP
    smem = pl.BlockSpec(memory_space=pltpu.SMEM)
    vmem = pl.BlockSpec(memory_space=pltpu.VMEM)
    hbm = pl.BlockSpec(memory_space=pl.ANY)
    out = jax.ShapeDtypeStruct((rows, width), F32)
    return pl.pallas_call(
        functools.partial(kernel, n_visit, n_patch),
        out_shape=(out, out),
        in_specs=[hbm] * 4 + [smem] * 7,
        out_specs=(vmem, vmem),
        scratch_shapes=[
            pltpu.VMEM(ccd_images.shape, BF16),
            pltpu.VMEM(warp_rows.shape, BF16),
            pltpu.VMEM(warp_cols.shape, BF16),
            pltpu.VMEM(psf_match.shape, BF16),
            pltpu.VMEM((ccd_images.shape[0] * K_OV, TS, TS), BF16),
            pltpu.SMEM((boxes,), jnp.int32),
            pltpu.SMEM((G,), F32),
            pltpu.VMEM((STEPS, boxes, high, TS), BF16),
            pltpu.VMEM((STEPS, boxes, high, TS), BF16),
            pltpu.VMEM((STEPS, n_visit, G, step_rows, TS), BF16),
            pltpu.VMEM((2, STEPS, n_visit, G, step_rows, TS), BF16),
            pltpu.VMEM((G * G, BAND, boxes * BAND), BF16),
            pltpu.VMEM((rows + 2 * EDGE_R, width + 2 * EDGE_C), F32),
            pltpu.SemaphoreType.DMA((4,)),
            pltpu.SemaphoreType.DMA((STEPS, n_patch - 1)),
            pltpu.SemaphoreType.DMA((STEPS, n_patch - 1)),
            pltpu.SemaphoreType.DMA((2, STEPS, n_visit)),
            pltpu.SemaphoreType.DMA((2, STEPS, n_visit)),
            pltpu.SemaphoreType.DMA((2, STEPS)),
            pltpu.SemaphoreType.DMA((2, STEPS)),
            pltpu.SemaphoreType.DMA((6,)),
            pltpu.SemaphoreType.DMA((6,)),
        ],
        compiler_params=pltpu.CompilerParams(
            collective_id=0, has_side_effects=True, vmem_limit_bytes=56 * 1024 * 1024
        ),
    )(
        ccd_images,
        warp_rows,
        warp_cols,
        psf_match,
        detect_kernel,
        ccd_weight,
        psf_index,
        patch_target[:, 0],
        tile_slot,
        row_matrix,
        col_matrix,
    )


def solution(mesh):
    in_specs = (P(("visit", "patch"), None, None), P(), P(), P(), P(), P(), P(), P(), P(), P(), P())
    out_specs = (P("visit", "patch"), P("visit", "patch"))
    return jax.shard_map(body, mesh=mesh, in_specs=in_specs, out_specs=out_specs, check_vma=False)
```

time: 95.8 us -> 71.9 us (0.75)
  Pallas kernels: 83.3 us -> 67.7 us
  local copies, waits for them, and re-layouts: 11.2 us -> 3.37 us
    pallas_call x1, Pallas kernels: 83.3 us -> 67.7 us  [body(): pl.pallas_call(functools.partial(kernel, n_visit, n_patch), out_shape=(ou...]
    unnamed x22 -> x4, local copies, waits for them, and re-layouts: 10.3 us -> 3.37 us
where the time goes in v2:
time: 71.9 us; the launch traced here: 71.7 us
  Pallas kernels  67.7 us (94%)
  local copies, waits for them, and re-layouts  3.37 us (5%)
    pallas_call x1, Pallas kernels, body(): pl.pallas_call(functools.partial(kernel, n_visit, n_patch), out_shape=(ou...  67.7 us
    unnamed x4, local copies, waits for them, and re-layouts  3.37 us

profile of v2, /device:TPU:1, one launch (start us, length us, event | category | flops | bytes accessed | tf_op | source)
XLA Modules:
  0.0 71.7 jit_solution(9494369196196576275)
XLA Ops:
  0.6 67.7 %shard_map.122 = (f32[256,1024]{1,0:T(8,128)}, f32[256,1024]{1,0:T(8,128)}) custom-call(bf16[4,512,256]{2,1,0:T(8,128)(2,1)} %images_hbm.1, bf16[8,256,512]{2,1,0:T(8,128)(2,1)} %rows_hbm.1, bf16[8,256,256]{2,1,0:T(8,128)(2,1)} %cols_hbm.1, bf16[8,256,256]{2,1,0:T(8,128)(2,1)} %psf_hbm.1, f32[9]{0:T(128)} %taps.1, f32[128]{0:T(128)} %weight.1, ...), custom_call_target="tpu_custom_call" | custom-call | tf_op jit(solution)/shard_map/pallas_call | solution.py:458
  68.3 0.0 copy-start
  68.4 2.4 %copy.15 = f32[256,1024]{1,0:T(8,128)} copy(f32[256,1024]{1,0:T(8,128)} %get-tuple-element.4) | data formatting | bytes 2097152
  70.8 0.0 copy-done
  70.8 1.0 %copy.16 = f32[256,1024]{1,0:T(8,128)} copy(f32[256,1024]{1,0:T(8,128)S(1)} %copy-done) | data formatting | bytes 2097152
Async XLA Ops:
  68.3 2.4 %copy-start = (f32[256,1024]{1,0:T(8,128)S(1)}, f32[256,1024]{1,0:T(8,128)}, u32[]{:S(2)}) copy-start(f32[256,1024]{1,0:T(8,128)} %get-tuple-element.5) | copy-start | bytes 3145732

commit v3 on v2

--- a/solution.py
+++ b/solution.py
@@ -13,6 +13,7 @@
 CAP = 2
 STEPS = 8
 AHEAD = 2
+LAG = 4
 BAND = 16
 EDGE_R = 8
 EDGE_C = 128
@@ -36,8 +37,7 @@
     slot,
     row_pick,
     col_pick,
-    coadd,
-    detection,
+    out,
     images,
     row_tables,
     col_tables,
@@ -51,7 +51,9 @@
     arrived,
     mix,
     ext,
+    filtered,
     load_sem,
+    o_sem,
     p_send,
     p_recv,
     v_send,
@@ -66,8 +68,8 @@
     n_images = images.shape[0]
     per_device = n_images * K_OV
     boxes = n_patch * CAP
-    rows = coadd.shape[0]
-    width = coadd.shape[1]
+    rows = out.shape[1]
+    width = out.shape[2]
     step_rows = rows // STEPS
     parts = TS // rows
     own = v * n_patch + p
@@ -225,16 +227,16 @@
         def _():
             pass_on(c, False, False)
 
-    def forward(c):
-        @pl.when(jnp.logical_and(v > 0, 2 * v < n_visit))
+    def forward(c, near):
+        low = 2 * v < n_visit
+
+        @pl.when(jnp.logical_and(v > 0, low if near else jnp.logical_not(low)))
         def _():
             pass_on(c, True, True)
+
+        @pl.when(jnp.logical_and(v < n_visit - 1, jnp.logical_not(low) if near else low))
+        def _():
             pass_on(c, False, True)
-
-        @pl.when(jnp.logical_and(v < n_visit - 1, 2 * v >= n_visit))
-        def _():
-            pass_on(c, False, True)
-            pass_on(c, True, True)
 
     def column_copy(c, k):
         at = pl.multiple_of(EDGE_R + c * step_rows, 8)
@@ -270,6 +272,14 @@
             device_id_type=MESH,
         )
 
+    def store(c, k):
+        at = pl.multiple_of(c * step_rows, step_rows)
+        if k == 0:
+            here = ext.at[pl.ds(pl.multiple_of(EDGE_R + at, 8), step_rows), pl.ds(EDGE_C, width)]
+        else:
+            here = filtered.at[pl.ds(at, step_rows)]
+        return pltpu.make_async_copy(here, out.at[k, pl.ds(at, step_rows)], o_sem.at[k, c])
+
     def finish(c):
         @pl.when(v > 0)
         def _():
@@ -285,8 +295,8 @@
             total = total + arrived[0, c, v, g].astype(F32)
             total = total + arrived[1, c, v, g].astype(F32)
             value = total * (1.0 / (1.0 + jnp.full((1, TS), slot_weight[g])))
-            coadd[pl.ds(at, step_rows), g * TS : (g + 1) * TS] = value
             ext[pl.ds(EDGE_R + at, step_rows), EDGE_C + g * TS : EDGE_C + (g + 1) * TS] = value
+        store(c, 0).start()
         for k in range(2):
 
             @pl.when(inside(0, -1 if k == 0 else 1))
@@ -321,10 +331,11 @@
             result = taps[0] * across[:, low : low + width]
             for j in range(1, count):
                 result = result + taps[j] * across[:, low + j : low + j + width]
-            detection[pl.ds(at, BAND), :] = result
+            filtered[pl.ds(at, BAND), :] = result
             return 0
 
         lax.fori_loop(0, step_rows // BAND, one, 0)
+        store(c, 1).start()
 
     pl.semaphore_wait(barrier, n_patch - 1 + 2 + len(corners))
     for c in range(AHEAD):
@@ -366,16 +377,17 @@
         carry = list(carry)
         for j in range(K_OV):
             e = i * K_OV + j
-            mine = target[e] == p
-            at = slot[e] - tile_row * G
+            at = jnp.where(target[e] == p, slot[e] - tile_row * G, -1)
             for g in range(G):
-                chosen = jnp.logical_and(mine, at == g)
-                carry[g] = carry[g] + jnp.where(chosen, weight[i], 0.0)
+                carry[g] = carry[g] + jnp.where(at == g, weight[i], 0.0)
         return tuple(carry)
 
-    totals = lax.fori_loop(0, weight.shape[0], tally, (jnp.float32(0),) * G)
-    for g in range(G):
-        slot_weight[g] = totals[g]
+    def count_weights(k):
+        half = weight.shape[0] // 2
+        totals = tuple(jnp.float32(0) if k == 0 else slot_weight[g] for g in range(G))
+        totals = lax.fori_loop(k * half, (k + 1) * half, tally, totals)
+        for g in range(G):
+            slot_weight[g] = totals[g]
 
     def stage(t, first, last, do):
         @pl.when(jnp.logical_and(t >= first, t <= last))
@@ -385,13 +397,16 @@
     def step(t, _):
         stage(t, 0, STEPS - 1 - AHEAD, lambda: send_patch(t + AHEAD))
         stage(t, 0, STEPS - 1, lambda: combine(t))
-        stage(t, 1, STEPS, lambda: forward(t - 1))
-        stage(t, 2, STEPS + 1, lambda: finish(t - 2))
-        stage(t, 3, STEPS + 2, lambda: columns_in(t - 3))
-        stage(t, 5, STEPS + 2, lambda: detect(t - 4))
+        stage(t, 1, STEPS, lambda: forward(t - 1, True))
+        stage(t, 2, STEPS + 1, lambda: forward(t - 2, False))
+        stage(t, 2, 2, lambda: count_weights(0))
+        stage(t, 3, 3, lambda: count_weights(1))
+        stage(t, LAG, STEPS + LAG - 1, lambda: finish(t - LAG))
+        stage(t, LAG + 1, STEPS + LAG, lambda: columns_in(t - LAG - 1))
+        stage(t, LAG + 3, STEPS + LAG, lambda: detect(t - LAG - 2))
         return 0
 
-    lax.fori_loop(0, STEPS + 3, step, 0)
+    lax.fori_loop(0, STEPS + LAG + 1, step, 0)
     for k, (dv, dp) in enumerate(around):
 
         @pl.when(inside(-dv, -dp))
@@ -410,6 +425,8 @@
     def drain(c, _):
         for d in range(1, n_patch):
             patch_copy(c, d).wait_send()
+        for k in range(2):
+            store(c, k).wait()
         for k in range(2):
 
             @pl.when(inside(0, -1 if k == 0 else 1))
@@ -452,14 +469,13 @@
     high = TS // rows * step_rows
     boxes = n_patch * CAP
     smem = pl.BlockSpec(memory_space=pltpu.SMEM)
-    vmem = pl.BlockSpec(memory_space=pltpu.VMEM)
     hbm = pl.BlockSpec(memory_space=pl.ANY)
-    out = jax.ShapeDtypeStruct((rows, width), F32)
-    return pl.pallas_call(
+    out = jax.ShapeDtypeStruct((2, rows, width), F32)
+    both = pl.pallas_call(
         functools.partial(kernel, n_visit, n_patch),
-        out_shape=(out, out),
+        out_shape=out,
         in_specs=[hbm] * 4 + [smem] * 7,
-        out_specs=(vmem, vmem),
+        out_specs=hbm,
         scratch_shapes=[
             pltpu.VMEM(ccd_images.shape, BF16),
             pltpu.VMEM(warp_rows.shape, BF16),
@@ -474,7 +490,9 @@
             pltpu.VMEM((2, STEPS, n_visit, G, step_rows, TS), BF16),
             pltpu.VMEM((G * G, BAND, boxes * BAND), BF16),
             pltpu.VMEM((rows + 2 * EDGE_R, width + 2 * EDGE_C), F32),
+            pltpu.VMEM((rows, width), F32),
             pltpu.SemaphoreType.DMA((4,)),
+            pltpu.SemaphoreType.DMA((2, STEPS)),
             pltpu.SemaphoreType.DMA((STEPS, n_patch - 1)),
             pltpu.SemaphoreType.DMA((STEPS, n_patch - 1)),
             pltpu.SemaphoreType.DMA((2, STEPS, n_visit)),
@@ -500,6 +518,7 @@
         row_matrix,
         col_matrix,
     )
+    return both[0], both[1]
 
 
 def solution(mesh):

time: 71.9 us -> 69.9 us (0.972)
  Pallas kernels: 67.7 us -> 66 us
    unnamed x4 -> x0, local copies, waits for them, and re-layouts: 3.37 us -> none
    squeeze x0 -> x1, local copies, waits for them, and re-layouts: none -> 3.11 us  [body(): return (both[0], both[1])]
    pallas_call x1, Pallas kernels: 67.7 us -> 66 us  [body(): pl.pallas_call(functools.partial(kernel, n_visit, n_patch), out_shape=out...]
where the time goes in v3:
time: 69.9 us; the launch traced here: 69.7 us
  Pallas kernels  66 us (94%)
  local copies, waits for them, and re-layouts  3.11 us (4%)
    pallas_call x1, Pallas kernels, body(): pl.pallas_call(functools.partial(kernel, n_visit, n_patch), out_shape=out...  66 us
    squeeze x1, local copies, waits for them, and re-layouts, body(): return (both[0], both[1])  3.11 us

profile of v3, /device:TPU:1, one launch (start us, length us, event | category | flops | bytes accessed | tf_op | source)
XLA Modules:
  0.0 69.7 jit_solution(8100846817412002592)
XLA Ops:
  0.6 66.0 %shard_map.122 = f32[2,256,1024]{2,1,0:T(8,128)} custom-call(bf16[4,512,256]{2,1,0:T(8,128)(2,1)} %images_hbm.1, bf16[8,256,512]{2,1,0:T(8,128)(2,1)} %rows_hbm.1, bf16[8,256,256]{2,1,0:T(8,128)(2,1)} %cols_hbm.1, bf16[8,256,256]{2,1,0:T(8,128)(2,1)} %psf_hbm.1, f32[9]{0:T(128)} %taps.1, f32[128]{0:T(128)} %weight.1, s32[128]{0:T(128)} %psf_index.1, ...), custom_call_target="tpu_custom_call" | custom-call | tf_op jit(solution)/shard_map/pallas_call | solution.py:474
  66.6 3.1 %slice_bitcast_fusion = (f32[256,1024]{1,0:T(8,128)}, f32[256,1024]{1,0:T(8,128)}) fusion(f32[2,256,1024]{2,1,0:T(8,128)} %shard_map.122), kind=kLoop, calls=%fused_computation | loop fusion | bytes 4194304 | tf_op jit(solution)/shard_map/squeeze | solution.py:521

commit v4 on v3

--- a/solution.py
+++ b/solution.py
@@ -12,8 +12,8 @@
 G = 4
 CAP = 2
 STEPS = 8
-AHEAD = 2
-LAG = 4
+AHEAD = 4
+LAG = 6
 BAND = 16
 EDGE_R = 8
 EDGE_C = 128
@@ -31,13 +31,20 @@
     cols_hbm,
     psf_hbm,
     taps,
+    weight_hbm,
+    psf_index_hbm,
+    target_hbm,
+    slot_hbm,
+    row_pick_hbm,
+    col_pick_hbm,
+    coadd,
+    detection,
     weight,
     psf_index,
     target,
     slot,
     row_pick,
     col_pick,
-    out,
     images,
     row_tables,
     col_tables,
@@ -68,20 +75,28 @@
     n_images = images.shape[0]
     per_device = n_images * K_OV
     boxes = n_patch * CAP
-    rows = out.shape[1]
-    width = out.shape[2]
+    rows = coadd.shape[0]
+    width = coadd.shape[1]
     step_rows = rows // STEPS
     parts = TS // rows
     own = v * n_patch + p
     base = own * per_device
 
+    lists = [
+        pltpu.make_async_copy(target_hbm, target, load_sem.at[4]),
+        pltpu.make_async_copy(slot_hbm, slot, load_sem.at[5]),
+        pltpu.make_async_copy(row_pick_hbm, row_pick, load_sem.at[6]),
+        pltpu.make_async_copy(col_pick_hbm, col_pick, load_sem.at[7]),
+        pltpu.make_async_copy(psf_index_hbm, psf_index, load_sem.at[8]),
+        pltpu.make_async_copy(weight_hbm, weight, load_sem.at[9]),
+    ]
     loads = [
         pltpu.make_async_copy(rows_hbm, row_tables, load_sem.at[0]),
         pltpu.make_async_copy(images_hbm, images, load_sem.at[1]),
         pltpu.make_async_copy(cols_hbm, col_tables, load_sem.at[2]),
         pltpu.make_async_copy(psf_hbm, psf_tables, load_sem.at[3]),
     ]
-    for load in loads:
+    for load in lists + loads:
         load.start()
 
     def entry_for(start, patch, rank):
@@ -124,6 +139,9 @@
                 continue
             ok = term if ok is None else jnp.logical_and(ok, term)
         return ok
+
+    for load in lists:
+        load.wait()
 
     def find(s, _):
         entry_of[s] = entry_for(base, s // CAP, lax.rem(s, CAP))[0]
@@ -278,7 +296,8 @@
             here = ext.at[pl.ds(pl.multiple_of(EDGE_R + at, 8), step_rows), pl.ds(EDGE_C, width)]
         else:
             here = filtered.at[pl.ds(at, step_rows)]
-        return pltpu.make_async_copy(here, out.at[k, pl.ds(at, step_rows)], o_sem.at[k, c])
+        out = coadd if k == 0 else detection
+        return pltpu.make_async_copy(here, out.at[pl.ds(at, step_rows)], o_sem.at[k, c])
 
     def finish(c):
         @pl.when(v > 0)
@@ -394,27 +413,30 @@
         def _():
             do()
 
+    lag = jnp.where(jnp.logical_or(v == 0, v == n_visit - 1), LAG, 2)
+
     def step(t, _):
         stage(t, 0, STEPS - 1 - AHEAD, lambda: send_patch(t + AHEAD))
         stage(t, 0, STEPS - 1, lambda: combine(t))
         stage(t, 1, STEPS, lambda: forward(t - 1, True))
         stage(t, 2, STEPS + 1, lambda: forward(t - 2, False))
-        stage(t, 2, 2, lambda: count_weights(0))
-        stage(t, 3, 3, lambda: count_weights(1))
-        stage(t, LAG, STEPS + LAG - 1, lambda: finish(t - LAG))
-        stage(t, LAG + 1, STEPS + LAG, lambda: columns_in(t - LAG - 1))
-        stage(t, LAG + 3, STEPS + LAG, lambda: detect(t - LAG - 2))
+        stage(t, 0, 0, lambda: count_weights(0))
+        stage(t, 1, 1, lambda: count_weights(1))
+        stage(t, lag, STEPS + lag - 1, lambda: finish(t - lag))
+        stage(t, lag + 1, STEPS + lag, lambda: columns_in(t - lag - 1))
+        stage(t, lag + 3, STEPS + lag, lambda: detect(t - lag - 2))
         return 0
 
     lax.fori_loop(0, STEPS + LAG + 1, step, 0)
-    for k, (dv, dp) in enumerate(around):
-
-        @pl.when(inside(-dv, -dp))
-        def _():
-            row_copy(k).wait_recv()
-
-    detect(STEPS - 1)
-    detect(0)
+    for edge, last in ((-1, STEPS - 1), (1, 0)):
+        for k, (dv, dp) in enumerate(around):
+            if dv == edge:
+
+                @pl.when(inside(-dv, -dp))
+                def _():
+                    row_copy(k).wait_recv()
+
+        detect(last)
 
     for k, (dv, dp) in enumerate(around):
 
@@ -470,13 +492,19 @@
     boxes = n_patch * CAP
     smem = pl.BlockSpec(memory_space=pltpu.SMEM)
     hbm = pl.BlockSpec(memory_space=pl.ANY)
-    out = jax.ShapeDtypeStruct((2, rows, width), F32)
-    both = pl.pallas_call(
+    out = jax.ShapeDtypeStruct((rows, width), F32)
+    return pl.pallas_call(
         functools.partial(kernel, n_visit, n_patch),
-        out_shape=out,
-        in_specs=[hbm] * 4 + [smem] * 7,
-        out_specs=hbm,
+        out_shape=(out, out),
+        in_specs=[hbm] * 4 + [smem] + [hbm] * 6,
+        out_specs=(hbm, hbm),
         scratch_shapes=[
+            pltpu.SMEM(ccd_weight.shape, F32),
+            pltpu.SMEM(psf_index.shape, jnp.int32),
+            pltpu.SMEM(tile_slot.shape, jnp.int32),
+            pltpu.SMEM(tile_slot.shape, jnp.int32),
+            pltpu.SMEM(row_matrix.shape, jnp.int32),
+            pltpu.SMEM(col_matrix.shape, jnp.int32),
             pltpu.VMEM(ccd_images.shape, BF16),
             pltpu.VMEM(warp_rows.shape, BF16),
             pltpu.VMEM(warp_cols.shape, BF16),
@@ -491,7 +519,7 @@
             pltpu.VMEM((G * G, BAND, boxes * BAND), BF16),
             pltpu.VMEM((rows + 2 * EDGE_R, width + 2 * EDGE_C), F32),
             pltpu.VMEM((rows, width), F32),
-            pltpu.SemaphoreType.DMA((4,)),
+            pltpu.SemaphoreType.DMA((10,)),
             pltpu.SemaphoreType.DMA((2, STEPS)),
             pltpu.SemaphoreType.DMA((STEPS, n_patch - 1)),
             pltpu.SemaphoreType.DMA((STEPS, n_patch - 1)),
@@ -503,7 +531,7 @@
             pltpu.SemaphoreType.DMA((6,)),
         ],
         compiler_params=pltpu.CompilerParams(
-            collective_id=0, has_side_effects=True, vmem_limit_bytes=56 * 1024 * 1024
+            collective_id=0, has_side_effects=True, vmem_limit_bytes=60 * 1024 * 1024
         ),
     )(
         ccd_images,
@@ -518,7 +546,6 @@
         row_matrix,
         col_matrix,
     )
-    return both[0], both[1]
 
 
 def solution(mesh):

time: 69.9 us -> 70.1 us (level)
    unnamed x0 -> x4, local copies, waits for them, and re-layouts: none -> 3.37 us
    squeeze x1 -> x0, local copies, waits for them, and re-layouts: 3.11 us -> none  [body(): return (both[0], both[1])]
where the time goes in v4:
time: 70.1 us; the launch traced here: 69.9 us
  Pallas kernels  65.9 us (94%)
  local copies, waits for them, and re-layouts  3.37 us (5%)
    pallas_call x1, Pallas kernels, body(): pl.pallas_call(functools.partial(kernel, n_visit, n_patch), out_shape=(ou...  65.9 us
    unnamed x4, local copies, waits for them, and re-layouts  3.37 us

profile of v4, /device:TPU:1, one launch (start us, length us, event | category | flops | bytes accessed | tf_op | source)
XLA Modules:
  0.0 69.9 jit_solution(8157216526818508829)
XLA Ops:
  0.6 65.9 %shard_map.122 = (f32[256,1024]{1,0:T(8,128)}, f32[256,1024]{1,0:T(8,128)}) custom-call(bf16[4,512,256]{2,1,0:T(8,128)(2,1)} %images_hbm.1, bf16[8,256,512]{2,1,0:T(8,128)(2,1)} %rows_hbm.1, bf16[8,256,256]{2,1,0:T(8,128)(2,1)} %cols_hbm.1, bf16[8,256,256]{2,1,0:T(8,128)(2,1)} %psf_hbm.1, f32[9]{0:T(128)} %taps.1, f32[128]{0:T(128)} %weight_hbm.1, ...), custom_call_target="tpu_custom_call" | custom-call | tf_op jit(solution)/shard_map/pallas_call | solution.py:496
  66.5 0.0 copy-start
  66.5 2.4 %copy.15 = f32[256,1024]{1,0:T(8,128)} copy(f32[256,1024]{1,0:T(8,128)} %get-tuple-element.4) | data formatting | bytes 2097152
  68.9 0.0 copy-done
  68.9 1.0 %copy.16 = f32[256,1024]{1,0:T(8,128)} copy(f32[256,1024]{1,0:T(8,128)S(1)} %copy-done) | data formatting | bytes 2097152
Async XLA Ops:
  66.5 2.4 %copy-start = (f32[256,1024]{1,0:T(8,128)S(1)}, f32[256,1024]{1,0:T(8,128)}, u32[]{:S(2)}) copy-start(f32[256,1024]{1,0:T(8,128)} %get-tuple-element.5) | copy-start | bytes 3145732
